TPU v7x, 32 devices: a whole 2x2x4 slice. The times are simulated.
32 devices in a mesh: depth: 4 (over z), probe: 8 (over y, x, core).
Axes of the slice: x: 2, y: 2, z: 4, core: 2. Of those that a mesh axis runs over, the one named last changes fastest.
Arguments:
- residual: bfloat16 [32, 2, 256, 256], P('probe'), may hold values from -4 to 4
- saved_waves: bfloat16 [8, 32, 2, 256, 256], P('depth', 'probe'), may hold values from -4 to 4
- object_phase: float32 [8, 384, 384], P('depth'), may hold values from -3.140625 to 3.140625
- object_amp: float32 [8, 384, 384], P('depth'), may hold values from 0.25 to 1.75
- prop_phase: float32 [256, 256], replicated, may hold values from -3.140625 to 3.140625
- offsets: int32 [32, 2], P('probe'), may hold values from 0 to 128
Outputs:
- object_grad: float32 [8, 2, 384, 384], P('depth', None, 'probe')
- probe_grad: float32 [2, 256, 256], P(None, 'probe', 'depth')
Inputs may be any that keep to these rules, and one draw needn't show every extreme that they name: `offsets`: every window lies inside the patch.
All inputs are finite; a program needn't handle non-finite values.
Results may differ from a plain program's by a relative error of at most 0.025.
The roundings to bfloat16 on the way count: a program that leaves them out, or rounds other values in their place, can miss the bound.
Values may be sent and summed in bfloat16 or wider, within the bound.
A program may use at most 128 MiB of HBM per device.

v0:
```python
import math

import jax
import jax.numpy as jnp
from jax import lax
from jax.sharding import PartitionSpec as P

MB_POS = 2


def passed_along(block, axis, distance):
    devices = range(lax.axis_size(axis))
    route = [(i - distance, i) for i in devices if i - distance in devices]
    return lax.ppermute(block, axis, route)


def from_root(value, axis, source):
    kept = jnp.where(lax.axis_index(axis) == source, value, 0).astype(value.dtype)
    return lax.psum(kept, axis)


def tables(width):
    rows = lax.broadcasted_iota(jnp.int32, (width, width), 0)
    cols = lax.broadcasted_iota(jnp.int32, (width, width), 1)
    phase = 2.0 * math.pi / width * (rows * cols % width).astype(jnp.float32)
    factor = 1.0 / math.sqrt(width)
    return (
        (jnp.cos(phase) * factor).astype(jnp.bfloat16),
        (jnp.sin(phase) * factor).astype(jnp.bfloat16),
    )


def left_first(real_part, imag_part, waves):
    block = jnp.concatenate(
        [jnp.concatenate([real_part, -imag_part], 1), jnp.concatenate([imag_part, real_part], 1)], 0
    )
    batch, _, width, _ = waves.shape
    flat = waves.reshape(batch, 2 * width, width)
    result = jnp.einsum("jk,bkl->bjl", block, flat, preferred_element_type=jnp.float32)
    return result.reshape(batch, 2, width, width)


def left_apply(real_part, imag_part, waves):
    block = jnp.concatenate(
        [jnp.concatenate([real_part, -imag_part], 1), jnp.concatenate([imag_part, real_part], 1)], 0
    )
    batch, _, width, _ = waves.shape
    flat = waves.reshape(batch, 2 * width, width)
    result = jnp.einsum(
        "jk,bkl->bjl", block.astype(jnp.float32), flat, precision=lax.Precision.HIGHEST
    )
    return result.reshape(batch, 2, width, width)


def right_apply(real_part, imag_part, waves):
    batch, _, width, _ = waves.shape
    real_table = real_part.astype(jnp.float32)
    imag_table = imag_part.astype(jnp.float32)
    wave_real = waves[:, 0].reshape(batch * width, width)
    wave_imag = waves[:, 1].reshape(batch * width, width)
    high = lax.Precision.HIGHEST
    out_real = jnp.dot(wave_real, real_table, precision=high) - jnp.dot(
        wave_imag, imag_table, precision=high
    )
    out_imag = jnp.dot(wave_real, imag_table, precision=high) + jnp.dot(
        wave_imag, real_table, precision=high
    )
    return jnp.stack([out_real, out_imag], 1).reshape(batch, 2, width, width)


def back_propagate(chi, cosine, sine, kernel_cos, kernel_sin):
    first = left_first(cosine, -sine, chi)
    spectrum = right_apply(cosine, -sine, first)
    spec_real = spectrum[:, 0]
    spec_imag = spectrum[:, 1]
    filtered = jnp.stack(
        [
            kernel_cos * spec_real + kernel_sin * spec_imag,
            kernel_cos * spec_imag - kernel_sin * spec_real,
        ],
        1,
    )
    second = left_apply(cosine, sine, filtered)
    return right_apply(cosine, sine, second)


def shards(residual, saved_waves, object_phase, object_amp, prop_phase, offsets):
    pos_count, _, width, _ = residual.shape
    section_count = lax.axis_size("depth")
    section_index = lax.axis_index("depth")
    cosine, sine = tables(width)
    kernel_cos = jnp.cos(prop_phase)
    kernel_sin = jnp.sin(prop_phase)
    transmission = jnp.stack(
        [object_amp * jnp.cos(object_phase), object_amp * jnp.sin(object_phase)], 1
    )
    zero_index = jnp.zeros((), jnp.int32)
    group_count = pos_count // MB_POS
    group_size = pos_count // group_count
    tick_count = section_count + group_count - 1

    def work(operands):
        incoming, grads, probe_sum, first = operands
        chi = incoming
        places = lax.dynamic_slice_in_dim(offsets, first, group_size, 0)
        row_starts = places[:, 0]
        col_starts = places[:, 1]
        for layer in (1, 0):
            arrived = back_propagate(chi, cosine, sine, kernel_cos, kernel_sin)
            chi_real = arrived[:, 0]
            chi_imag = arrived[:, 1]
            waves = lax.dynamic_slice_in_dim(saved_waves[layer], first, group_size, 0).astype(
                jnp.float32
            )
            psi_real = waves[:, 0]
            psi_imag = waves[:, 1]
            terms = jnp.stack(
                [
                    psi_real * chi_real + psi_imag * chi_imag,
                    psi_real * chi_imag - psi_imag * chi_real,
                ],
                1,
            )

            def deposit(position, layer_grad):
                corner = (zero_index, row_starts[position], col_starts[position])
                window = lax.dynamic_slice(layer_grad, corner, (2, width, width))
                return lax.dynamic_update_slice(layer_grad, window + terms[position], corner)

            layer_grad = lax.fori_loop(0, group_size, deposit, grads[layer])
            grads = grads.at[layer].set(layer_grad)
            layer_trans = transmission[layer]
            windows = jax.vmap(
                lambda row_at, col_at: lax.dynamic_slice(
                    layer_trans, (zero_index, row_at, col_at), (2, width, width)
                )
            )(row_starts, col_starts)
            trans_real = windows[:, 0]
            trans_imag = windows[:, 1]
            chi = jnp.stack(
                [
                    trans_real * chi_real + trans_imag * chi_imag,
                    trans_real * chi_imag - trans_imag * chi_real,
                ],
                1,
            ).astype(jnp.bfloat16)
        probe_sum = probe_sum + jnp.sum(chi.astype(jnp.float32), axis=0)
        return (chi, grads, probe_sum)

    def skip(operands):
        incoming, grads, probe_sum, first = operands
        return (jnp.zeros_like(incoming), grads, probe_sum)

    def tick(tick_now, carry):
        inbox, grads, probe_sum = carry
        group_now = tick_now - (section_count - 1 - section_index)
        active = (group_now >= 0) & (group_now < group_count)
        first = jnp.clip(group_now, 0, group_count - 1) * group_size
        fresh = lax.dynamic_slice_in_dim(residual, first, group_size, 0)
        incoming = jnp.where(section_index == section_count - 1, fresh, inbox)
        outgoing, grads, probe_sum = lax.cond(
            active, work, skip, (incoming, grads, probe_sum, first)
        )
        inbox = passed_along(outgoing, "depth", -1)
        return (inbox, grads, probe_sum)

    patch = object_phase.shape[-1]
    start_inbox = jnp.zeros((group_size, 2, width, width), jnp.bfloat16)
    start_grads = jnp.zeros((object_phase.shape[0], 2, patch, patch), jnp.float32)
    start_probe = jnp.zeros((2, width, width), jnp.float32)
    _, grads, probe_sum = lax.fori_loop(
        0, tick_count, tick, (start_inbox, start_grads, start_probe)
    )
    object_grad = lax.psum_scatter(grads, "probe", scatter_dimension=2, tiled=True)
    total = lax.psum(probe_sum, "probe")
    rows_each = width // lax.axis_size("probe")
    own_rows = lax.dynamic_slice_in_dim(total, lax.axis_index("probe") * rows_each, rows_each, 1)
    spread_rows = from_root(own_rows, "depth", 0)
    cols_each = width // section_count
    probe_grad = lax.dynamic_slice_in_dim(spread_rows, section_index * cols_each, cols_each, 2)
    return (object_grad, probe_grad)


def solution(mesh):
    return jax.shard_map(
        shards,
        mesh=mesh,
        in_specs=(
            P("probe", None, None, None),
            P("depth", "probe", None, None, None),
            P("depth", None, None),
            P("depth", None, None),
            P(),
            P("probe", None),
        ),
        out_specs=(P("depth", None, "probe", None), P(None, "probe", "depth")),
        check_vma=False,
    )
```

profile of v0, /device:TPU:0, one launch (start us, length us, event | category | flops | bytes accessed | tf_op | source)
XLA Modules:
  0.0 814.2 jit_solution(11077362429882749235)
XLA Ops:
  10.5 6.7 multiply_bitcast_fusion.1
  21.3 650.3 %while.61 = (s32[]{:T(128)}, bf16[2,2,256,256]{3,2,1,0:T(8,128)(2,1)S(1)}, f32[2,2,384,384]{3,2,1,0:T(8,128)}, f32[2,256,256]{2,1,0:T(8,128)}, s32[]{:T(128)}, /...) while((s32[]{:T(128)}, ...), condition=%wide.region_8.9_spmd.clone.clone, body=%wide.region_0.8_spmd.clone.clone.sunk | while | flops 10220994560 | bytes 155455280 | solution.py:171
  24.6 15.8 %collective-permute-done = bf16[2,2,256,256]{3,2,1,0:T(8,128)(2,1)S(1)} collective-permute-done((bf16[2,2,256,256]{3,2,1,0:T(8,128)(2,1)}, bf16[2,2,256,256]{3,2,1,0:T(8,128)(2,1)S(1)}, u32[]{:S(2)}, u32[]{:S(2)}) %collective-permute-start) | collective-permute-done | bytes 524320 | tf_op jit(solution)/shard_map/while/body/eval_jaxpr/ppermute | solution.py:14
  43.6 13.9 %collective-permute-done = bf16[2,2,256,256]{3,2,1,0:T(8,128)(2,1)S(1)} collective-permute-done((bf16[2,2,256,256]{3,2,1,0:T(8,128)(2,1)}, bf16[2,2,256,256]{3,2,1,0:T(8,128)(2,1)S(1)}, u32[]{:S(2)}, u32[]{:S(2)}) %collective-permute-start) | collective-permute-done | bytes 524320 | tf_op jit(solution)/shard_map/while/body/eval_jaxpr/ppermute | solution.py:14
  60.8 352.7 %collective-permute-done = bf16[2,2,256,256]{3,2,1,0:T(8,128)(2,1)S(1)} collective-permute-done((bf16[2,2,256,256]{3,2,1,0:T(8,128)(2,1)}, bf16[2,2,256,256]{3,2,1,0:T(8,128)(2,1)S(1)}, u32[]{:S(2)}, u32[]{:S(2)}) %collective-permute-start) | collective-permute-done | bytes 524320 | tf_op jit(solution)/shard_map/while/body/eval_jaxpr/ppermute | solution.py:14
  414.6 114.0 %conditional.4 = (bf16[2,2,256,256]{3,2,1,0:T(8,128)(2,1)}, f32[2,2,384,384]{3,2,1,0:T(8,128)}, f32[2,256,256]{2,1,0:T(8,128)}) conditional(s32[]{:T(128)} %convert_element_type.189, (f32[2,2,384,384]{3,2,1,0:T(8,128)}, f32[2,256,256]{2,1,0:T(8,128)}) %tuple.173, (f32[2,2,384,384]{3,2,1,0:T(8,128)}, s32[]{:T(128)}, s32[4,2]{1,0:T(4,128)S(1)}, ...), branch_computations={%region_1.1_spmd, %region_2.7_spmd} | conditional | flops 10219814912 | bytes 153095456 | solution.py:161
  433.8 7.9 while.60
  452.9 25.1 %while.57 = (s32[]{:T(128)}, f32[2,384,384]{2,1,0:T(8,128)S(1)}, s32[2]{0:T(128)S(1)}, s32[2]{0:T(128)S(1)}, f32[2,2,256,256]{3,2,1,0:T(8,128)S(1)}, /*index=5*/s32[]{:T(128)}, s32[]{:T(128)}, s32[]{:T(128)}) while((s32[]{:T(128)}, f32[2,384,384]{2,1,0:T(8,128)S(1)}, s32[2]{0:T(128)S(1)}, s32[2]{0:T(128)S(1)}, ...), condition=%wide.region_4.3_spmd, body=%wide.region_3.2_spmd.sunk | while | flops 131080 | bytes 2621641 | solution.py:130
  458.1 8.1 dynamic_update_slice.16
  502.3 25.2 %while.58 = (s32[]{:T(128)}, f32[2,384,384]{2,1,0:T(8,128)S(1)}, s32[2]{0:T(128)S(1)}, s32[2]{0:T(128)S(1)}, f32[2,2,256,256]{3,2,1,0:T(8,128)S(1)}, /*index=5*/s32[]{:T(128)}, s32[]{:T(128)}, s32[]{:T(128)}) while((s32[]{:T(128)}, f32[2,384,384]{2,1,0:T(8,128)S(1)}, s32[2]{0:T(128)S(1)}, s32[2]{0:T(128)S(1)}, ...), condition=%wide.region_6.5_spmd, body=%wide.region_5.4_spmd.sunk | while | flops 131080 | bytes 2621641 | solution.py:130
  507.6 8.1 dynamic_update_slice.17
  529.9 13.3 %collective-permute-done = bf16[2,2,256,256]{3,2,1,0:T(8,128)(2,1)S(1)} collective-permute-done((bf16[2,2,256,256]{3,2,1,0:T(8,128)(2,1)}, bf16[2,2,256,256]{3,2,1,0:T(8,128)(2,1)S(1)}, u32[]{:S(2)}, u32[]{:S(2)}) %collective-permute-start) | collective-permute-done | bytes 524320 | tf_op jit(solution)/shard_map/while/body/eval_jaxpr/ppermute | solution.py:14
  544.3 116.0 %conditional.4 = (bf16[2,2,256,256]{3,2,1,0:T(8,128)(2,1)}, f32[2,2,384,384]{3,2,1,0:T(8,128)}, f32[2,256,256]{2,1,0:T(8,128)}) conditional(s32[]{:T(128)} %convert_element_type.189, (f32[2,2,384,384]{3,2,1,0:T(8,128)}, f32[2,256,256]{2,1,0:T(8,128)}) %tuple.173, (f32[2,2,384,384]{3,2,1,0:T(8,128)}, s32[]{:T(128)}, s32[4,2]{1,0:T(4,128)S(1)}, ...), branch_computations={%region_1.1_spmd, %region_2.7_spmd} | conditional | flops 10219814912 | bytes 153095456 | solution.py:161
  563.5 7.9 while.60
  582.6 26.0 %while.57 = (s32[]{:T(128)}, f32[2,384,384]{2,1,0:T(8,128)S(1)}, s32[2]{0:T(128)S(1)}, s32[2]{0:T(128)S(1)}, f32[2,2,256,256]{3,2,1,0:T(8,128)S(1)}, /*index=5*/s32[]{:T(128)}, s32[]{:T(128)}, s32[]{:T(128)}) while((s32[]{:T(128)}, f32[2,384,384]{2,1,0:T(8,128)S(1)}, s32[2]{0:T(128)S(1)}, s32[2]{0:T(128)S(1)}, ...), condition=%wide.region_4.3_spmd, body=%wide.region_3.2_spmd.sunk | while | flops 131080 | bytes 2621641 | solution.py:130
  587.8 8.0 dynamic_update_slice.16
  601.1 7.6 dynamic_update_slice.16
  633.0 26.2 %while.58 = (s32[]{:T(128)}, f32[2,384,384]{2,1,0:T(8,128)S(1)}, s32[2]{0:T(128)S(1)}, s32[2]{0:T(128)S(1)}, f32[2,2,256,256]{3,2,1,0:T(8,128)S(1)}, /*index=5*/s32[]{:T(128)}, s32[]{:T(128)}, s32[]{:T(128)}) while((s32[]{:T(128)}, f32[2,384,384]{2,1,0:T(8,128)S(1)}, s32[2]{0:T(128)S(1)}, s32[2]{0:T(128)S(1)}, ...), condition=%wide.region_6.5_spmd, body=%wide.region_5.4_spmd.sunk | while | flops 131080 | bytes 2621641 | solution.py:130
  638.3 8.0 dynamic_update_slice.17
  651.6 7.6 dynamic_update_slice.17
  661.6 10.0 %collective-permute-done = bf16[2,2,256,256]{3,2,1,0:T(8,128)(2,1)S(1)} collective-permute-done((bf16[2,2,256,256]{3,2,1,0:T(8,128)(2,1)}, bf16[2,2,256,256]{3,2,1,0:T(8,128)(2,1)S(1)}, u32[]{:S(2)}, u32[]{:S(2)}) %collective-permute-start) | collective-permute-done | bytes 524320 | tf_op jit(solution)/shard_map/while/body/eval_jaxpr/ppermute | solution.py:14
  671.7 54.1 %all-reduce.3.cloned.1.call-done = f32[2,256,256]{2,1,0:T(8,128)} async-done(((f32[2,256,256]{2,1,0:T(8,128)}), f32[2,256,256]{2,1,0:T(8,128)}) %all-reduce.3.cloned.1.call-update) | async-done | bytes 524304 | tf_op jit(solution)/shard_map/psum | solution.py:175
  728.0 33.5 %all-reduce.5.cloned.1.call-done = f32[2,32,256]{2,1,0:T(8,128)} async-done(((f32[2,32,256]{2,1,0:T(8,128)}), f32[2,32,256]{2,1,0:T(8,128)}) %all-reduce.5.cloned.1.call-update) | async-done | bytes 65552 | tf_op jit(solution)/shard_map/psum | solution.py:19
  763.0 44.7 %reduce-scatter.2.cloned.1.call-done = f32[2,2,48,384]{3,2,1,0:T(8,128)} async-done(((f32[2,2,384,384]{3,2,1,0:T(8,128)}), f32[2,2,48,384]{3,2,1,0:T(8,128)}) %reduce-scatter.2.cloned.1.call-update) | async-done | bytes 294928 | tf_op jit(solution)/shard_map/reduce_scatter | solution.py:174
  (248 shorter events, 191.2 us)
Async XLA Ops:
  7.2 718.6 %all-reduce.3.cloned.1.call-start = ((), (), s32[]{:S(2)}) async-start(), calls=%async_computation.2 | async-start | bytes 1048576 | tf_op jit(solution)/shard_map/psum | solution.py:175
  23.3 17.0 %collective-permute-start = (bf16[2,2,256,256]{3,2,1,0:T(8,128)(2,1)}, bf16[2,2,256,256]{3,2,1,0:T(8,128)(2,1)S(1)}, u32[]{:S(2)}, u32[]{:S(2)}) collective-permute-start(bf16[2,2,256,256]{3,2,1,0:T(8,128)(2,1)} %get-tuple-element.1183), channel_id=1, source_target_pairs={{8,0},{16,8},{24,16},{9,1},{17,9},{25,17},{10,2},{18,10},{26,18},{... | collective-permute-start | bytes 1572872 | tf_op jit(solution)/shard_map/while/body/eval_jaxpr/ppermute | solution.py:14
  42.3 15.2 %collective-permute-start = (bf16[2,2,256,256]{3,2,1,0:T(8,128)(2,1)}, bf16[2,2,256,256]{3,2,1,0:T(8,128)(2,1)S(1)}, u32[]{:S(2)}, u32[]{:S(2)}) collective-permute-start(bf16[2,2,256,256]{3,2,1,0:T(8,128)(2,1)} %get-tuple-element.1183), channel_id=1, source_target_pairs={{8,0},{16,8},{24,16},{9,1},{17,9},{25,17},{10,2},{18,10},{26,18},{... | collective-permute-start | bytes 1572872 | tf_op jit(solution)/shard_map/while/body/eval_jaxpr/ppermute | solution.py:14
  59.5 354.0 %collective-permute-start = (bf16[2,2,256,256]{3,2,1,0:T(8,128)(2,1)}, bf16[2,2,256,256]{3,2,1,0:T(8,128)(2,1)S(1)}, u32[]{:S(2)}, u32[]{:S(2)}) collective-permute-start(bf16[2,2,256,256]{3,2,1,0:T(8,128)(2,1)} %get-tuple-element.1183), channel_id=1, source_target_pairs={{8,0},{16,8},{24,16},{9,1},{17,9},{25,17},{10,2},{18,10},{26,18},{... | collective-permute-start | bytes 1572872 | tf_op jit(solution)/shard_map/while/body/eval_jaxpr/ppermute | solution.py:14
  415.0 1.7 copy-start.5
  415.0 6.2 copy-start.3
  450.6 1.6 copy-start.1
  450.6 1.9 copy-start.2
  486.0 0.9 copy-start.4
  493.4 1.7 copy-start
  528.6 14.6 %collective-permute-start = (bf16[2,2,256,256]{3,2,1,0:T(8,128)(2,1)}, bf16[2,2,256,256]{3,2,1,0:T(8,128)(2,1)S(1)}, u32[]{:S(2)}, u32[]{:S(2)}) collective-permute-start(bf16[2,2,256,256]{3,2,1,0:T(8,128)(2,1)} %get-tuple-element.1183), channel_id=1, source_target_pairs={{8,0},{16,8},{24,16},{9,1},{17,9},{25,17},{10,2},{18,10},{26,18},{... | collective-permute-start | bytes 1572872 | tf_op jit(solution)/shard_map/while/body/eval_jaxpr/ppermute | solution.py:14
  544.7 1.7 copy-start.5
  544.7 6.2 copy-start.3
  580.3 1.6 copy-start.1
  580.3 1.9 copy-start.2
  616.7 0.9 copy-start.4
  624.1 1.7 copy-start
  660.3 11.3 %collective-permute-start = (bf16[2,2,256,256]{3,2,1,0:T(8,128)(2,1)}, bf16[2,2,256,256]{3,2,1,0:T(8,128)(2,1)S(1)}, u32[]{:S(2)}, u32[]{:S(2)}) collective-permute-start(bf16[2,2,256,256]{3,2,1,0:T(8,128)(2,1)} %get-tuple-element.1183), channel_id=1, source_target_pairs={{8,0},{16,8},{24,16},{9,1},{17,9},{25,17},{10,2},{18,10},{26,18},{... | collective-permute-start | bytes 1572872 | tf_op jit(solution)/shard_map/while/body/eval_jaxpr/ppermute | solution.py:14
  671.6 89.9 %all-reduce.5.cloned.1.call-start = ((), (), s32[]{:S(2)}) async-start(), calls=%async_computation.3 | async-start | bytes 131072 | tf_op jit(solution)/shard_map/psum | solution.py:19
  727.3 80.4 %reduce-scatter.2.cloned.1.call-start = ((), (), s32[]{:S(2)}) async-start(), calls=%async_computation.1 | async-start | bytes 2654208 | tf_op jit(solution)/shard_map/reduce_scatter | solution.py:174
Sparse Core Ops, SparseCore 0:
  671.7 54.0 all-reduce.2
  728.2 33.2 all-reduce.4
  765.5 42.1 reduce-scatter.1
where the time goes:
time: 818 us; the launch traced here: 814 us
  waiting for transfers between devices  539 us (66%)
  local copies, waits for them, and re-layouts  162 us (20%)
  other arithmetic  37.9 us (5%)
  loops' own time  31.8 us (4%)
  matrix products  23.4 us (3%)
  between operations  13.8 us (2%)
    ppermute x5, waiting for transfers between devices, passed_along(): return lax.ppermute(block, axis, route)  406 us
    dynamic_update_slice x8, local copies, waits for them, and re-layouts, deposit(): lax.dynamic_update_slice(layer_grad, window + terms[position], corner)  60.5 us
    psum x1, waiting for transfers between devices, shards(): total = lax.psum(probe_sum, 'probe')  54.1 us
    reduce_scatter x1, waiting for transfers between devices, shards(): lax.psum_scatter(grads, 'probe', scatter_dimension=2, tiled=True)  44.7 us
    psum x1, waiting for transfers between devices, from_root(): return lax.psum(kept, axis)  33.5 us
    another operation x4, loops' own time, work(): layer_grad = lax.fori_loop(0, group_size, deposit, grads[layer])  30.5 us
    gather x24, local copies, waits for them, and re-layouts  27.9 us
  transfers between devices with their start and end apart: 8, of which 8 were waited for; matrix products, arithmetic and copies ran while one was open for 0% of the time, Pallas kernels for 0%

commit v1 on v0

v1 whole, which is shorter than its diff:
```python
import functools
import math

import jax
import jax.numpy as jnp
import ml_dtypes
import numpy as np
from jax import lax
from jax.experimental import pallas as pl
from jax.experimental.pallas import tpu as pltpu
from jax.sharding import PartitionSpec as P

LANES = 128
SUBLANES = 8
VMEM_BYTES = 56 * 1024 * 1024


def half_tables(width):
    half = width // 2
    at = np.arange(width)
    phase = 2.0 * math.pi / width * (np.outer(at, at) % width)
    cosine = np.cos(phase) / math.sqrt(width)
    sine = np.sin(phase) / math.sqrt(width)
    blocks = []
    for parity in (0, 1):
        c, s = cosine[:half, parity::2], sine[:half, parity::2]
        blocks.append(np.block([[c, s], [-s, c]]))
    for parity in (0, 1):
        c, s = cosine[:half, parity::2], sine[:half, parity::2]
        blocks.append(np.block([[c, -s], [s, c]]))
    for parity in (0, 1):
        c, s = cosine[parity::2, :half], sine[parity::2, :half]
        blocks.append(np.block([[c, s], [-s, c]]))
    return np.stack(blocks).astype(np.float32).astype(ml_dtypes.bfloat16)


def order_table(width):
    order = np.concatenate([np.arange(0, width, 2), np.arange(1, width, 2)])
    table = np.zeros((width, width), np.float32)
    table[np.arange(width), order] = 1.0
    return table


def rows(*blocks):
    return jnp.concatenate(blocks, 0)


def cols(*blocks):
    return jnp.concatenate(blocks, 1)


def dot(a, b):
    return jnp.dot(a, b, preferred_element_type=jnp.float32)


def back_propagate(x_real, x_imag, tables, kernel_cos, kernel_sin):
    half = x_real.shape[0] // 2
    low = jnp.bfloat16
    spans = (slice(0, half), slice(half, 2 * half))
    even = dot(tables[0], rows(x_real[:half], x_imag[:half]))
    odd = dot(tables[1], rows(x_real[half:], x_imag[half:]))
    sums, gaps = [], []
    for part in (even + odd, even - odd):
        left, right = part[:, :half], part[:, half:]
        total, gap = (left + right).astype(low), (left - right).astype(low)
        sums.append(cols(total[:half], total[half:]))
        gaps.append(cols(gap[:half], gap[half:]))
    spec_even = dot(rows(*sums), tables[2])
    spec_odd = dot(rows(*gaps), tables[3])
    parts = []
    for parity in spans:
        z_real, z_imag = [], []
        for at, spec in zip(spans, (spec_even, spec_odd)):
            real, imag = spec[:half, parity], spec[half:, parity]
            kc, ks = kernel_cos[parity, at], kernel_sin[parity, at]
            z_real.append((kc * real + ks * imag).astype(low))
            z_imag.append((kc * imag - ks * real).astype(low))
        parts.append(rows(cols(*z_real), cols(*z_imag)))
    even, odd = dot(tables[2], parts[0]), dot(tables[3], parts[1])
    top, bottom = (even + odd).astype(low), (even - odd).astype(low)
    ends = []
    for at, span in enumerate(spans):
        block = rows(
            cols(top[:half, span], top[half:, span]),
            cols(bottom[:half, span], bottom[half:, span]),
        )
        ends.append(dot(block, tables[4 + at]))
    sides = ends[0] + ends[1], ends[0] - ends[1]
    return [[(side[:half, parity], side[half:, parity]) for side in sides] for parity in spans]


def tile_rows(block):
    return block.reshape(block.shape[0] // SUBLANES, SUBLANES, block.shape[1])


def rows_earlier(block, count):
    tiles = pltpu.roll(tile_rows(block), lax.rem(SUBLANES - count, SUBLANES), 1)
    near = lax.broadcasted_iota(jnp.int32, tiles[1:].shape, 1) < SUBLANES - count
    kept = jnp.where(near, tiles[:-1], tiles[1:])
    return kept.reshape(block.shape[0] - SUBLANES, block.shape[1])


def rows_later(block, count):
    tiles = pltpu.roll(tile_rows(block), count, 1)
    zero = jnp.zeros_like(tiles[:1])
    below, above = rows(tiles, zero), rows(zero, tiles)
    far = lax.broadcasted_iota(jnp.int32, below.shape, 1) >= count
    return jnp.where(far, below, above).reshape(block.shape[0] + SUBLANES, block.shape[1])


def adjoint_kernel(
    place_ref,
    offsets_ref,
    residual_ref,
    waves_ref,
    trans_ref,
    phase_ref,
    tables_ref,
    order_ref,
    grads_ref,
    probe_ref,
    chi,
    layer_trans,
    kernel_cos,
    kernel_sin,
    totals,
    woven,
):
    positions, _, width, _ = residual_ref.shape
    sections, bands, own, _, band_rows, patch = trans_ref.shape
    section = place_ref[0]
    order = order_ref[...]
    exact = functools.partial(
        lax.dot_general, precision=lax.Precision.HIGHEST, preferred_element_type=jnp.float32
    )
    ordered = exact(order, phase_ref[...], (((1,), (0,)), ((), ())))
    ordered = exact(ordered, order, (((1,), (1,)), ((), ())))
    kernel_cos[...] = jnp.cos(ordered)
    kernel_sin[...] = jnp.sin(ordered)
    totals[...] = jnp.zeros_like(totals)
    half = width // 2
    split = order.astype(jnp.bfloat16)
    for position in range(positions):
        for part in (0, 1):
            chi[position, part] = dot(split, residual_ref[position, part]).astype(chi.dtype)
    lane = lax.broadcasted_iota(jnp.int32, (half + SUBLANES, LANES), 1)
    spans = (slice(0, LANES), slice(LANES, 2 * LANES), slice(2 * LANES, 3 * LANES))

    def layer_step(at_section, layer, deposit):
        for part in (0, 1):
            for band in range(bands):
                block = trans_ref[at_section, band, layer, part].astype(jnp.float32)
                count = band_rows // 2
                for parity in (0, 1):
                    layer_trans[part, parity, pl.ds(band * count, count), :] = block[
                        parity * count : (parity + 1) * count
                    ]
        for position in range(positions):
            row_at = offsets_ref[position, 0]
            col_at = offsets_ref[position, 1]
            into = lax.rem(LANES - col_at, LANES)
            outof = lax.rem(col_at, LANES)
            behind = lane < LANES - col_at
            ahead = lane >= col_at
            tables = [tables_ref[k] for k in range(6)]
            q = back_propagate(
                chi[position, 0], chi[position, 1], tables, kernel_cos, kernel_sin
            )
            if deposit:
                psi = [dot(split, waves_ref[layer, position, part]) for part in (0, 1)]
            for parity in (0, 1):
                first = (row_at + parity) // 2
                plane = lax.rem(row_at + parity, 2)
                rest = lax.rem(first, SUBLANES)
                window = pl.ds(pl.multiple_of(first - rest, SUBLANES), half + SUBLANES)
                own_rows = slice(parity * half, (parity + 1) * half)
                if deposit:
                    terms = ([], [])
                    for at in (0, 1):
                        real, imag = q[parity][at]
                        psi_real, psi_imag = (plane_of[own_rows, spans[at]] for plane_of in psi)
                        pair = psi_real * real + psi_imag * imag, psi_real * imag - psi_imag * real
                        for part in (0, 1):
                            terms[part].append(
                                pltpu.roll(rows_later(pair[part], rest), outof, 1)
                            )
                    for part in (0, 1):
                        left, right = terms[part]
                        shifted = (
                            jnp.where(ahead, left, 0.0),
                            jnp.where(ahead, right, left),
                            jnp.where(ahead, 0.0, right),
                        )
                        for at in range(3):
                            totals[layer, part, plane, window, spans[at]] += shifted[at]
                trans = []
                for part in (0, 1):
                    tiles = [
                        pltpu.roll(layer_trans[part, plane, window, spans[at]], into, 1)
                        for at in range(3)
                    ]
                    trans.append(
                        [
                            rows_earlier(jnp.where(behind, tiles[at], tiles[at + 1]), rest)
                            for at in (0, 1)
                        ]
                    )
                for at in (0, 1):
                    real, imag = q[parity][at]
                    tr, ti = trans[0][at], trans[1][at]
                    chi[position, 0, own_rows, spans[at]] = (tr * real + ti * imag).astype(chi.dtype)
                    chi[position, 1, own_rows, spans[at]] = (tr * imag - ti * real).astype(chi.dtype)

    def deeper(step, carry):
        index = sections * own - 1 - step
        layer_step(index // own, lax.rem(index, own), False)
        return carry

    lax.fori_loop(0, (sections - 1 - section) * own, deeper, 0)

    def mine(step, carry):
        layer_step(section, own - 1 - step, True)
        return carry

    lax.fori_loop(0, own, mine, 0)
    for part in (0, 1):
        for layer in range(own):
            for at, span in enumerate(spans):
                for parity in (0, 1):
                    woven[at, pl.ds(parity, patch // 2, 2), :] = totals[
                        layer, part, parity, : patch // 2, span
                    ]
                grads_ref[layer, part, :, span] = woven[at]
        for parity in (0, 1):
            own_rows = slice(parity * half, (parity + 1) * half)
            total = chi[0, part, own_rows].astype(jnp.float32)
            for position in range(1, positions):
                total = total + chi[position, part, own_rows].astype(jnp.float32)
            total = jnp.where(section == 0, total, 0.0)
            for at, span in enumerate(spans[:2]):
                woven[at, pl.ds(parity, half, 2), :] = total[:, span]
        for at, span in enumerate(spans[:2]):
            probe_ref[part, :, span] = woven[at, :width]


def shards(residual, saved_waves, object_phase, object_amp, prop_phase, offsets):
    positions, _, width, _ = residual.shape
    own, patch, _ = object_phase.shape
    sections = lax.axis_size("depth")
    bands = lax.axis_size("probe")
    section = lax.axis_index("depth")
    band_rows = patch // bands
    assert width == 2 * LANES and patch == 3 * LANES

    start = lax.axis_index("probe") * band_rows
    phase = lax.dynamic_slice_in_dim(object_phase, start, band_rows, 1)
    amp = lax.dynamic_slice_in_dim(object_amp, start, band_rows, 1)
    share = jnp.stack([amp * jnp.cos(phase), amp * jnp.sin(phase)], 1).astype(jnp.bfloat16)
    share = share.reshape(own, 2, band_rows // 2, 2, patch).swapaxes(2, 3)
    share = share.reshape(own, 2, band_rows, patch)
    trans = lax.all_gather(share, ("depth", "probe"))
    trans = trans.reshape((sections, bands) + share.shape)

    vmem = pl.BlockSpec(memory_space=pltpu.VMEM)
    smem = pl.BlockSpec(memory_space=pltpu.SMEM)
    grads, probe_sum = pl.pallas_call(
        adjoint_kernel,
        out_shape=(
            jax.ShapeDtypeStruct((own, 2, patch, patch), jnp.float32),
            jax.ShapeDtypeStruct((2, width, width), jnp.float32),
        ),
        in_specs=[smem, smem] + [vmem] * 6,
        out_specs=(vmem, vmem),
        scratch_shapes=[
            pltpu.VMEM(residual.shape, jnp.bfloat16),
            pltpu.VMEM((2, 2, patch // 2 + SUBLANES, patch), jnp.float32),
            pltpu.VMEM((width, width), jnp.float32),
            pltpu.VMEM((width, width), jnp.float32),
            pltpu.VMEM((own, 2, 2, patch // 2 + SUBLANES, patch), jnp.float32),
            pltpu.VMEM((3, patch, LANES), jnp.float32),
        ],
        compiler_params=pltpu.CompilerParams(vmem_limit_bytes=VMEM_BYTES),
        name="adjoint",
    )(
        section.astype(jnp.int32)[None],
        offsets,
        residual,
        saved_waves,
        trans,
        prop_phase,
        jnp.asarray(half_tables(width)),
        jnp.asarray(order_table(width)),
    )
    object_grad = lax.psum_scatter(grads, "probe", scatter_dimension=2, tiled=True)
    rows_each, cols_each = width // bands, width // sections
    blocks = probe_sum.reshape(2, bands, rows_each, sections, cols_each)
    blocks = blocks.transpose(1, 3, 0, 2, 4).reshape(bands * sections, 2, rows_each, cols_each)
    probe_grad = lax.psum_scatter(blocks, ("probe", "depth"), scatter_dimension=0, tiled=False)
    return (object_grad, probe_grad)


def solution(mesh):
    return jax.shard_map(
        shards,
        mesh=mesh,
        in_specs=(
            P("probe", None, None, None),
            P("depth", "probe", None, None, None),
            P("depth", None, None),
            P("depth", None, None),
            P(),
            P("probe", None),
        ),
        out_specs=(P("depth", None, "probe", None), P(None, "probe", "depth")),
        check_vma=False,
    )
```

time: 818 us -> 297 us (0.36)
  waiting for transfers between devices: 539 us -> 244 us
  local copies, waits for them, and re-layouts: 162 us -> 3.36 us
  other arithmetic: 37.9 us -> 2.21 us
  Pallas kernels: 0 us -> 33.5 us
  loops' own time: 31.8 us -> 0 us
  matrix products: 23.4 us -> 0 us
    ppermute x5 -> x0, waiting for transfers between devices: 406 us -> none  [passed_along(): return lax.ppermute(block, axis, route)]
    reduce_scatter x0 -> x1, waiting for transfers between devices: none -> 132 us  [shards(): lax.psum_scatter(blocks, ('probe', 'depth'), scatter_dimension=0, tiled=F...]
    psum x2 -> x0, waiting for transfers between devices: 87.6 us -> none  [the longest x1 54.1 us: shards(): total = lax.psum(probe_sum, 'probe')]
    all_gather x0 -> x1, waiting for transfers between devices: none -> 67.6 us  [shards(): trans = lax.all_gather(share, ('depth', 'probe'))]
    dynamic_update_slice x8 -> x0, local copies, waits for them, and re-layouts: 60.5 us -> none  [deposit(): lax.dynamic_update_slice(layer_grad, window + terms[position], corner)]
    pallas_call x0 -> x1, Pallas kernels: none -> 33.5 us  [shards(): pl.pallas_call(adjoint_kernel, out_shape=(jax.ShapeDtypeStruct((own, 2, p...]
    another operation x14 -> x0, loops' own time: 31.8 us -> none  [the longest x4 30.5 us: work(): layer_grad = lax.fori_loop(0, group_size, deposit, grads[layer])]
    gather x24 -> x0, local copies, waits for them, and re-layouts: 27.9 us -> none
  transfers between devices with their start and end apart: 8 -> 3, of which waited for: 8 -> 3; matrix products, arithmetic and copies ran while one was open for 0% -> 0% of each run, Pallas kernels for 0% -> 0%
where the time goes in v1:
time: 297 us
  waiting for transfers between devices  244 us (82%)
  Pallas kernels  33.5 us (11%)
  between operations  13.8 us (5%)
  local copies, waits for them, and re-layouts  3.36 us (1%)
    reduce_scatter x1, waiting for transfers between devices, shards(): lax.psum_scatter(blocks, ('probe', 'depth'), scatter_dimension=0, tiled=F...  132 us
    all_gather x1, waiting for transfers between devices, shards(): trans = lax.all_gather(share, ('depth', 'probe'))  67.6 us
    reduce_scatter x1, waiting for transfers between devices, shards(): lax.psum_scatter(grads, 'probe', scatter_dimension=2, tiled=True)  43.7 us
    pallas_call x1, Pallas kernels, shards(): pl.pallas_call(adjoint_kernel, out_shape=(jax.ShapeDtypeStruct((own, 2, p...  33.5 us
  transfers between devices with their start and end apart: 3, of which 3 were waited for; matrix products, arithmetic and copies ran while one was open for 0% of the time, Pallas kernels for 0%

profile of v1, /device:TPU:0, one launch (start us, length us, event | category | flops | bytes accessed | tf_op | source)
XLA Modules:
  0.0 297.1 jit_solution(18068324174780342863)
XLA Ops:
  7.2 0.0 copy-start
  7.2 0.0 all-gather.2.cloned.1.call-start
  7.2 1.5 multiply_convert_fusion.1
  8.9 0.7 pad_maximum_fusion
  9.6 0.0 all-gather.2.cloned.1.call-update
  9.6 0.0 reduce-scatter.5.cloned.1.call-start
  9.6 0.0 copy-done
  9.6 0.7 copy.15.offsets_ref
  10.3 67.6 %all-gather.2.cloned.1.call-done = bf16[32,2,2,48,384]{4,3,2,1,0:T(8,128)(2,1)} async-done(((bf16[1,2,2,48,384]{4,3,2,1,0:T(8,128)(2,1)}), bf16[32,2,2,48,384]{4,3,2,1,0:T(8,128)(2,1)}) %all-gather.2.cloned.1.call-update) | async-done | bytes 4718608 | tf_op jit(solution)/shard_map/all_gather | solution.py:261
  77.9 33.5 %adjoint.1 = (f32[2,2,384,384]{3,2,1,0:T(8,128)}, f32[2,256,256]{2,1,0:T(8,128)}) custom-call(s32[1]{0:T(128)} %bitcast.place_ref, s32[4,2]{1,0:T(4,128)} %copy.15.offsets_ref, bf16[4,2,256,256]{3,2,1,0:T(8,128)(2,1)} %residual_ref.1, bf16[2,4,2,256,256]{4,3,2,1,0:T(8,128)(2,1)} %waves_ref.1, bf16[4,8,2,2,48,384]{5,4,3,2,1,0:T(8,128)(2,1)} %bitcast.8, ...), custom_call_target="tpu_custom_call" | custom-call | tf_op jit(solution)/shard_map/adjoint/pallas_call | solution.py:266
  111.3 1.5 reshape.21
  112.8 1.1 copy.16
  113.9 0.0 reduce-scatter.5.cloned.1.call-update
  114.0 0.0 reduce-scatter.3.cloned.1.call-start
  114.0 0.7 reduce-scatter.3.cloned.1.call-update
  114.7 132.1 %reduce-scatter.5.cloned.1.call-done = f32[1,2,32,64]{3,2,1,0:T(8,128)} async-done(((f32[32,2,32,64]{3,2,1,0:T(8,128)}), f32[1,2,32,64]{3,2,1,0:T(8,128)}) %reduce-scatter.5.cloned.1.call-update) | async-done | bytes 16400 | tf_op jit(solution)/shard_map/reduce_scatter | solution.py:298
  246.8 43.7 %reduce-scatter.3.cloned.1.call-done = f32[2,2,48,384]{3,2,1,0:T(8,128)} async-done(((f32[2,2,384,384]{3,2,1,0:T(8,128)}), f32[2,2,48,384]{3,2,1,0:T(8,128)}) %reduce-scatter.3.cloned.1.call-update) | async-done | bytes 294928 | tf_op jit(solution)/shard_map/reduce_scatter | solution.py:294
  (4 shorter events, 0.1 us)
Async XLA Ops:
  7.2 2.5 copy-start
  7.2 70.7 %all-gather.2.cloned.1.call-start = ((), (), s32[]{:S(2)}) async-start(), calls=%async_computation.2 | async-start | bytes 4866048 | tf_op jit(solution)/shard_map/all_gather | solution.py:261
  9.6 237.3 %reduce-scatter.5.cloned.1.call-start = ((), (), s32[]{:S(2)}) async-start(), calls=%async_computation.4 | async-start | bytes 1081344 | tf_op jit(solution)/shard_map/reduce_scatter | solution.py:298
  114.0 176.6 %reduce-scatter.3.cloned.1.call-start = ((), (), s32[]{:S(2)}) async-start(), calls=%async_computation.3 | async-start | bytes 2654208 | tf_op jit(solution)/shard_map/reduce_scatter | solution.py:294
Sparse Core Ops, SparseCore 0:
  11.5 66.3 all-gather.1
  114.1 132.7 reduce-scatter.4
  251.1 39.3 reduce-scatter.2

commit v2 on v1

--- a/solution.py
+++ b/solution.py
@@ -230,17 +230,259 @@
                     woven[at, pl.ds(parity, patch // 2, 2), :] = totals[
                         layer, part, parity, : patch // 2, span
                     ]
-                grads_ref[layer, part, :, span] = woven[at]
+                for band in range(bands):
+                    grads_ref[band, layer, part, :, span] = woven[
+                        at, band * band_rows : (band + 1) * band_rows
+                    ].astype(grads_ref.dtype)
         for parity in (0, 1):
             own_rows = slice(parity * half, (parity + 1) * half)
             total = chi[0, part, own_rows].astype(jnp.float32)
             for position in range(1, positions):
                 total = total + chi[position, part, own_rows].astype(jnp.float32)
-            total = jnp.where(section == 0, total, 0.0)
             for at, span in enumerate(spans[:2]):
                 woven[at, pl.ds(parity, half, 2), :] = total[:, span]
         for at, span in enumerate(spans[:2]):
-            probe_ref[part, :, span] = woven[at, :width]
+            for band in range(bands):
+                count = width // bands
+                probe_ref[band, part, :, span] = woven[
+                    at, band * count : (band + 1) * count
+                ].astype(probe_ref.dtype)
+
+
+MESH = pl.DeviceIdType.MESH
+
+
+def partners(section, band, sections, bands):
+    chips = bands // 2
+    chip, core = band // 2, band % 2
+    found = [(section, 2 * chip + 1 - core)]
+    found += [(section, 2 * ((chip + j) % chips) + core) for j in range(1, chips)]
+    found += [((section + j) % sections, band) for j in range(1, sections)]
+    return found
+
+
+def meet(section, band, sections, bands):
+    barrier = pltpu.get_barrier_semaphore()
+    others = partners(section, band, sections, bands)
+    for other in others:
+        pl.semaphore_signal(barrier, inc=1, device_id=other, device_id_type=MESH)
+    pl.semaphore_wait(barrier, len(others))
+
+
+def gather_kernel(
+    sections,
+    bands,
+    share_ref,
+    trans_ref,
+    local_sem,
+    down_send,
+    down_recv,
+    plane_send,
+    plane_recv,
+    pair_send,
+    pair_recv,
+):
+    section, band = lax.axis_index("depth"), lax.axis_index("probe")
+    chips = bands // 2
+    chip, core = band // 2, band % 2
+    meet(section, band, sections, bands)
+
+    def send(source, slot, to, send_sem, recv_sem):
+        return pltpu.make_async_remote_copy(
+            src_ref=source,
+            dst_ref=trans_ref.at[slot],
+            send_sem=send_sem,
+            recv_sem=recv_sem,
+            device_id=to,
+            device_id_type=MESH,
+        )
+
+    def down(target, origin):
+        return send(
+            share_ref, (origin, band), (target, band), down_send.at[target], down_recv.at[origin]
+        )
+
+    def across(origin, j, source):
+        return send(
+            source,
+            (origin, band),
+            (section, 2 * ((chip + j) % chips) + core),
+            plane_send.at[origin, j],
+            plane_recv.at[origin, j],
+        )
+
+    def to_pair(origin, j, source):
+        slot = (origin, 2 * ((chip + chips - j) % chips) + core)
+        return send(
+            source if j == 0 else trans_ref.at[slot],
+            slot,
+            (section, 2 * chip + 1 - core),
+            pair_send.at[origin, j],
+            pair_recv.at[origin, j],
+        )
+
+    for target in range(sections - 1):
+
+        @pl.when(section > target)
+        def _(target=target):
+            down(target, section).start()
+
+    own_copy = pltpu.make_async_copy(share_ref, trans_ref.at[section, band], local_sem)
+    own_copy.start()
+    for j in range(1, chips):
+        across(section, j, share_ref).start()
+    to_pair(section, 0, share_ref).start()
+    for origin in range(1, sections):
+
+        @pl.when(section < origin)
+        def _(origin=origin):
+            down(0, origin).wait_recv()
+            held = trans_ref.at[origin, band]
+            for j in range(1, chips):
+                across(origin, j, held).start()
+            to_pair(origin, 0, held).start()
+
+    for origin in range(sections):
+
+        @pl.when(section <= origin)
+        def _(origin=origin):
+            for j in range(1, chips):
+                across(origin, j, share_ref).wait_recv()
+                to_pair(origin, j, None).start()
+
+    for origin in range(sections):
+
+        @pl.when(section <= origin)
+        def _(origin=origin):
+            for j in range(chips):
+                to_pair(origin, j, share_ref).wait()
+                if j:
+                    across(origin, j, share_ref).wait_send()
+
+    for target in range(sections - 1):
+
+        @pl.when(section > target)
+        def _(target=target):
+            down(target, section).wait_send()
+
+    own_copy.wait()
+
+
+def scatter_kernel(
+    sections,
+    bands,
+    grads_ref,
+    probe_ref,
+    object_out,
+    probe_out,
+    pair_g,
+    sum_g,
+    in_g,
+    pair_p,
+    sum_p,
+    in_p,
+    pieces,
+    arrived,
+    pair_send,
+    pair_recv,
+    plane_send,
+    plane_recv,
+    column_send,
+    column_recv,
+):
+    section, band = lax.axis_index("depth"), lax.axis_index("probe")
+    chips = bands // 2
+    chip, core = band // 2, band % 2
+    wide = jnp.float32
+    meet(section, band, sections, bands)
+    fields = ((probe_ref, pair_p, sum_p, in_p), (grads_ref, pair_g, sum_g, in_g))
+
+    def chip_at(j):
+        return (chip + j) % chips
+
+    def to_pair(field, j):
+        source, pair, _, _ = fields[field]
+        return pltpu.make_async_remote_copy(
+            src_ref=source.at[2 * chip_at(j) + 1 - core],
+            dst_ref=pair.at[j],
+            send_sem=pair_send.at[field, j],
+            recv_sem=pair_recv.at[field, j],
+            device_id=(section, 2 * chip + 1 - core),
+            device_id_type=MESH,
+        )
+
+    def across(field, j):
+        _, _, sums, into = fields[field]
+        return pltpu.make_async_remote_copy(
+            src_ref=sums.at[j],
+            dst_ref=into.at[j],
+            send_sem=plane_send.at[field, j],
+            recv_sem=plane_recv.at[field, j],
+            device_id=(section, 2 * chip_at(j) + core),
+            device_id_type=MESH,
+        )
+
+    def up(target):
+        return pltpu.make_async_remote_copy(
+            src_ref=pieces.at[target],
+            dst_ref=arrived,
+            send_sem=column_send.at[target],
+            recv_sem=column_recv,
+            device_id=(target, band),
+            device_id_type=MESH,
+        )
+
+    order = list(range(1, chips)) + [0]
+
+    def begin(field):
+        for j in order:
+            to_pair(field, j).start()
+
+    def pass_on(field):
+        source, pair, sums, _ = fields[field]
+        for j in order:
+            to_pair(field, j).wait()
+            both = source[2 * chip_at(j) + core].astype(wide) + pair[j].astype(wide)
+            if j == 0:
+                return both
+            sums[j] = both.astype(sums.dtype)
+            across(field, j).start()
+
+    def finish(field, both):
+        _, _, _, into = fields[field]
+        for j in range(1, chips):
+            across(field, j).wait()
+            both = both + into[j].astype(wide)
+        return both
+
+    @pl.when(section == 0)
+    def _():
+        begin(0)
+
+    begin(1)
+
+    @pl.when(section == 0)
+    def _():
+        total = finish(0, pass_on(0))
+        each = total.shape[-1] // sections
+        for target in range(sections):
+            pieces[target] = total[:, :, target * each : (target + 1) * each]
+        for target in range(1, sections):
+            up(target).start()
+        probe_out[...] = pieces[0]
+
+    object_out[...] = pass_on(1)
+    object_out[...] = finish(1, object_out[...])
+
+    @pl.when(section == 0)
+    def _():
+        for target in range(1, sections):
+            up(target).wait_send()
+
+    @pl.when(section > 0)
+    def _():
+        up(1).wait_recv()
+        probe_out[...] = arrived[...]
 
 
 def shards(residual, saved_waves, object_phase, object_amp, prop_phase, offsets):
@@ -250,6 +492,7 @@
     bands = lax.axis_size("probe")
     section = lax.axis_index("depth")
     band_rows = patch // bands
+    chips = bands // 2
     assert width == 2 * LANES and patch == 3 * LANES
 
     start = lax.axis_index("probe") * band_rows
@@ -258,16 +501,35 @@
     share = jnp.stack([amp * jnp.cos(phase), amp * jnp.sin(phase)], 1).astype(jnp.bfloat16)
     share = share.reshape(own, 2, band_rows // 2, 2, patch).swapaxes(2, 3)
     share = share.reshape(own, 2, band_rows, patch)
-    trans = lax.all_gather(share, ("depth", "probe"))
-    trans = trans.reshape((sections, bands) + share.shape)
 
     vmem = pl.BlockSpec(memory_space=pltpu.VMEM)
     smem = pl.BlockSpec(memory_space=pltpu.SMEM)
+    anywhere = pl.BlockSpec(memory_space=pl.ANY)
+    dma = pltpu.SemaphoreType.DMA
+    trans = pl.pallas_call(
+        functools.partial(gather_kernel, sections, bands),
+        out_shape=jax.ShapeDtypeStruct((sections, bands) + share.shape, jnp.bfloat16),
+        in_specs=[anywhere],
+        out_specs=anywhere,
+        scratch_shapes=[
+            dma,
+            dma((sections,)),
+            dma((sections,)),
+            dma((sections, chips)),
+            dma((sections, chips)),
+            dma((sections, chips)),
+            dma((sections, chips)),
+        ],
+        compiler_params=pltpu.CompilerParams(collective_id=0, has_side_effects=True),
+        name="gather",
+    )(share)
+
+    rows_each, cols_each = width // bands, width // sections
     grads, probe_sum = pl.pallas_call(
         adjoint_kernel,
         out_shape=(
-            jax.ShapeDtypeStruct((own, 2, patch, patch), jnp.float32),
-            jax.ShapeDtypeStruct((2, width, width), jnp.float32),
+            jax.ShapeDtypeStruct((bands, own, 2, band_rows, patch), jnp.bfloat16),
+            jax.ShapeDtypeStruct((bands, 2, rows_each, width), jnp.bfloat16),
         ),
         in_specs=[smem, smem] + [vmem] * 6,
         out_specs=(vmem, vmem),
@@ -291,12 +553,33 @@
         jnp.asarray(half_tables(width)),
         jnp.asarray(order_table(width)),
     )
-    object_grad = lax.psum_scatter(grads, "probe", scatter_dimension=2, tiled=True)
-    rows_each, cols_each = width // bands, width // sections
-    blocks = probe_sum.reshape(2, bands, rows_each, sections, cols_each)
-    blocks = blocks.transpose(1, 3, 0, 2, 4).reshape(bands * sections, 2, rows_each, cols_each)
-    probe_grad = lax.psum_scatter(blocks, ("probe", "depth"), scatter_dimension=0, tiled=False)
-    return (object_grad, probe_grad)
+    block_g, block_p = (own, 2, band_rows, patch), (2, rows_each, width)
+    low = jnp.bfloat16
+    return pl.pallas_call(
+        functools.partial(scatter_kernel, sections, bands),
+        out_shape=(
+            jax.ShapeDtypeStruct(block_g, jnp.float32),
+            jax.ShapeDtypeStruct((2, rows_each, cols_each), jnp.float32),
+        ),
+        in_specs=[vmem, vmem],
+        out_specs=(vmem, vmem),
+        scratch_shapes=[pltpu.VMEM((chips,) + block_g, low)] * 3
+        + [pltpu.VMEM((chips,) + block_p, low)] * 3
+        + [
+            pltpu.VMEM((sections, 2, rows_each, cols_each), jnp.float32),
+            pltpu.VMEM((2, rows_each, cols_each), jnp.float32),
+            dma((2, chips)),
+            dma((2, chips)),
+            dma((2, chips)),
+            dma((2, chips)),
+            dma((sections,)),
+            dma,
+        ],
+        compiler_params=pltpu.CompilerParams(
+            collective_id=1, has_side_effects=True, vmem_limit_bytes=VMEM_BYTES
+        ),
+        name="scatter",
+    )(grads, probe_sum)
 
 
 def solution(mesh):

time: 297 us -> 96.5 us (0.32)
  waiting for transfers between devices: 244 us -> 0 us
  Pallas kernels: 33.5 us -> 88.8 us
  between operations: 13.8 us -> 0.68 us
    reduce_scatter x2 -> x0, waiting for transfers between devices: 176 us -> none  [the longest x1 132 us: shards(): lax.psum_scatter(blocks, ('probe', 'depth'), scatter_dimension=0, tiled=F...]
    all_gather x1 -> x0, waiting for transfers between devices: 67.6 us -> none  [shards(): trans = lax.all_gather(share, ('depth', 'probe'))]
    pallas_call x1 -> x3, Pallas kernels: 33.5 us -> 88.8 us  [the longest x1 38.4 us: shards(): pl.pallas_call(functools.partial(gather_kernel, sections, bands), out_sha...]
    unnamed x3, local copies, waits for them, and re-layouts: 0.67 us -> 4.41 us
  transfers between devices with their start and end apart: 3 -> 0, of which waited for: 3 -> 0; matrix products, arithmetic and copies ran while one was open for 0% -> 0% of each run, Pallas kernels for 0% -> 0%
where the time goes in v2:
time: 96.5 us; the launch traced here: 96.2 us
  Pallas kernels  88.8 us (92%)
  local copies, waits for them, and re-layouts  4.49 us (5%)
  other arithmetic  2.2 us (2%)
    pallas_call x1, Pallas kernels, shards(): pl.pallas_call(functools.partial(gather_kernel, sections, bands), out_sha...  38.4 us
    pallas_call x1, Pallas kernels, shards(): pl.pallas_call(adjoint_kernel, out_shape=(jax.ShapeDtypeStruct((bands, ow...  33 us
    pallas_call x1, Pallas kernels, shards(): pl.pallas_call(functools.partial(scatter_kernel, sections, bands), out_sh...  17.3 us
    unnamed x3, local copies, waits for them, and re-layouts  4.41 us

profile of v2, /device:TPU:0, one launch (start us, length us, event | category | flops | bytes accessed | tf_op | source)
XLA Modules:
  0.0 96.2 jit_solution(9327721641614706925)
XLA Ops:
  0.6 1.3 %copy.12.offsets_ref = s32[4,2]{1,0:T(4,128)} copy(s32[4,2]{0,1:T(2,128)} %param.13) | data formatting | bytes 64 | tf_op args[5]
  2.0 1.5 %multiply_convert_fusion.1 = (bf16[2,48,384]{2,1,0:T(8,128)(2,1)S(1)}, bf16[2,48,384]{2,1,0:T(8,128)(2,1)S(1)}) fusion(f32[2,384,384]{2,1,0:T(8,128)} %param.10, s32[]{:T(128)S(6)} %select_n.4, f32[2,384,384]{2,1,0:T(8,128)} %param.11), kind=kLoop, calls=%fused_computation.2 | loop fusion | flops 147456 | bytes 442372 | tf_op jit(solution)/shard_map/convert.3
  3.6 0.7 pad_maximum_fusion
  4.3 38.4 %gather.1.trans_ref = bf16[4,8,2,2,48,384]{5,4,3,2,1,0:T(8,128)(2,1)} custom-call(bf16[2,2,48,384]{3,2,1,0:T(8,128)(2,1)} %bitcast.4), custom_call_target="tpu_custom_call" | custom-call | tf_op jit(solution)/shard_map/gather/pallas_call | solution.py:509
  42.7 33.0 %adjoint.1 = (bf16[8,2,2,48,384]{4,3,2,1,0:T(8,128)(2,1)}, bf16[8,2,32,256]{3,2,1,0:T(8,128)(2,1)}) custom-call(s32[1]{0:T(128)} %bitcast.place_ref, s32[4,2]{1,0:T(4,128)} %copy.12.offsets_ref, bf16[4,2,256,256]{3,2,1,0:T(8,128)(2,1)} %residual_ref.1, bf16[2,4,2,256,256]{4,3,2,1,0:T(8,128)(2,1)} %waves_ref.1, ...), custom_call_target="tpu_custom_call" | custom-call | tf_op jit(solution)/shard_map/adjoint/pallas_call | solution.py:528
  75.7 17.3 %scatter.1 = (f32[2,2,48,384]{3,2,1,0:T(8,128)}, f32[2,32,64]{2,1,0:T(8,128)}) custom-call(bf16[8,2,2,48,384]{4,3,2,1,0:T(8,128)(2,1)} %get-tuple-element.4.grads_ref, bf16[8,2,32,256]{3,2,1,0:T(8,128)(2,1)} %get-tuple-element.5.probe_ref), custom_call_target="tpu_custom_call" | custom-call | tf_op jit(solution)/shard_map/scatter/pallas_call | solution.py:558
  93.1 1.7 %copy.15 = f32[2,2,48,384]{3,2,1,0:T(8,128)} copy(f32[2,2,48,384]{3,2,1,0:T(8,128)} %get-tuple-element.10) | data formatting | bytes 589824
  94.8 1.4 %copy.16 = f32[2,32,64]{2,1,0:T(8,128)} copy(f32[2,32,64]{2,1,0:T(8,128)} %get-tuple-element.11) | data formatting | bytes 32768
  (4 shorter events, 0.1 us)

commit v3 on v2

--- a/solution.py
+++ b/solution.py
@@ -38,7 +38,7 @@
     order = np.concatenate([np.arange(0, width, 2), np.arange(1, width, 2)])
     table = np.zeros((width, width), np.float32)
     table[np.arange(width), order] = 1.0
-    return table
+    return table.astype(ml_dtypes.bfloat16)
 
 
 def rows(*blocks):
@@ -108,95 +108,88 @@
     return jnp.where(far, below, above).reshape(block.shape[0] + SUBLANES, block.shape[1])
 
 
-def adjoint_kernel(
-    place_ref,
+def cos_sin(angle):
+    part = angle * 0.5
+    square = part * part
+
+    def series(first, count):
+        terms = [(-1.0) ** k / math.factorial(2 * k + first) for k in range(count)]
+        total = jnp.full_like(square, terms[-1])
+        for term in terms[-2::-1]:
+            total = total * square + term
+        return total
+
+    sine, cosine = part * series(1, 7), series(0, 8)
+    return 1.0 - 2.0 * sine * sine, 2.0 * sine * cosine
+
+
+def spans_of(count):
+    return tuple(slice(k * LANES, (k + 1) * LANES) for k in range(count))
+
+
+def layer_step(position, chi, tables_ref, kernel_cos, kernel_sin, trans_of, deposit=None):
+    half = chi.shape[2] // 2
+    spans = spans_of(2)
+    tables = [tables_ref[k] for k in range(6)]
+    q = back_propagate(chi[position, 0], chi[position, 1], tables, kernel_cos, kernel_sin)
+    for parity in (0, 1):
+        own_rows = slice(parity * half, (parity + 1) * half)
+        if deposit is not None:
+            deposit(q[parity], parity)
+        trans = trans_of(parity)
+        for at in (0, 1):
+            real, imag = q[parity][at]
+            tr, ti = trans[0][at], trans[1][at]
+            chi[position, 0, own_rows, spans[at]] = (tr * real + ti * imag).astype(chi.dtype)
+            chi[position, 1, own_rows, spans[at]] = (tr * imag - ti * real).astype(chi.dtype)
+
+
+def own_kernel(
     offsets_ref,
-    residual_ref,
+    chi_ref,
     waves_ref,
     trans_ref,
-    phase_ref,
+    kernel_cos,
+    kernel_sin,
     tables_ref,
     order_ref,
     grads_ref,
     probe_ref,
     chi,
-    layer_trans,
-    kernel_cos,
-    kernel_sin,
     totals,
     woven,
 ):
-    positions, _, width, _ = residual_ref.shape
-    sections, bands, own, _, band_rows, patch = trans_ref.shape
-    section = place_ref[0]
-    order = order_ref[...]
-    exact = functools.partial(
-        lax.dot_general, precision=lax.Precision.HIGHEST, preferred_element_type=jnp.float32
-    )
-    ordered = exact(order, phase_ref[...], (((1,), (0,)), ((), ())))
-    ordered = exact(ordered, order, (((1,), (1,)), ((), ())))
-    kernel_cos[...] = jnp.cos(ordered)
-    kernel_sin[...] = jnp.sin(ordered)
+    positions, _, width, _ = chi_ref.shape
+    bands, own, _, band_rows, patch = grads_ref.shape
+    half = width // 2
+    split = order_ref[...]
+    spans = spans_of(3)
     totals[...] = jnp.zeros_like(totals)
-    half = width // 2
-    split = order.astype(jnp.bfloat16)
-    for position in range(positions):
-        for part in (0, 1):
-            chi[position, part] = dot(split, residual_ref[position, part]).astype(chi.dtype)
-    lane = lax.broadcasted_iota(jnp.int32, (half + SUBLANES, LANES), 1)
-    spans = (slice(0, LANES), slice(LANES, 2 * LANES), slice(2 * LANES, 3 * LANES))
-
-    def layer_step(at_section, layer, deposit):
-        for part in (0, 1):
-            for band in range(bands):
-                block = trans_ref[at_section, band, layer, part].astype(jnp.float32)
-                count = band_rows // 2
-                for parity in (0, 1):
-                    layer_trans[part, parity, pl.ds(band * count, count), :] = block[
-                        parity * count : (parity + 1) * count
-                    ]
+    chi[...] = chi_ref[...]
+
+    def mine(step, carry):
+        layer = own - 1 - step
+        lane = lax.broadcasted_iota(jnp.int32, (half + SUBLANES, LANES), 1)
         for position in range(positions):
+            psi = [dot(split, waves_ref[layer, position, part]) for part in (0, 1)]
             row_at = offsets_ref[position, 0]
             col_at = offsets_ref[position, 1]
-            into = lax.rem(LANES - col_at, LANES)
-            outof = lax.rem(col_at, LANES)
-            behind = lane < LANES - col_at
-            ahead = lane >= col_at
-            tables = [tables_ref[k] for k in range(6)]
-            q = back_propagate(
-                chi[position, 0], chi[position, 1], tables, kernel_cos, kernel_sin
-            )
-            if deposit:
-                psi = [dot(split, waves_ref[layer, position, part]) for part in (0, 1)]
-            for parity in (0, 1):
+
+            def place(parity, row_at=row_at):
                 first = (row_at + parity) // 2
                 plane = lax.rem(row_at + parity, 2)
                 rest = lax.rem(first, SUBLANES)
-                window = pl.ds(pl.multiple_of(first - rest, SUBLANES), half + SUBLANES)
-                own_rows = slice(parity * half, (parity + 1) * half)
-                if deposit:
-                    terms = ([], [])
-                    for at in (0, 1):
-                        real, imag = q[parity][at]
-                        psi_real, psi_imag = (plane_of[own_rows, spans[at]] for plane_of in psi)
-                        pair = psi_real * real + psi_imag * imag, psi_real * imag - psi_imag * real
-                        for part in (0, 1):
-                            terms[part].append(
-                                pltpu.roll(rows_later(pair[part], rest), outof, 1)
-                            )
-                    for part in (0, 1):
-                        left, right = terms[part]
-                        shifted = (
-                            jnp.where(ahead, left, 0.0),
-                            jnp.where(ahead, right, left),
-                            jnp.where(ahead, 0.0, right),
-                        )
-                        for at in range(3):
-                            totals[layer, part, plane, window, spans[at]] += shifted[at]
+                start = pl.multiple_of(first - rest, SUBLANES)
+                return plane, pl.ds(start, half + SUBLANES), rest
+
+            def trans_of(parity, place=place, col_at=col_at):
+                plane, window, rest = place(parity)
+                into = lax.rem(LANES - col_at, LANES)
+                behind = lane < LANES - col_at
                 trans = []
                 for part in (0, 1):
                     tiles = [
-                        pltpu.roll(layer_trans[part, plane, window, spans[at]], into, 1)
+                        pltpu.roll(trans_ref[layer, part, plane, window, spans[at]], into, 1)
                         for at in range(3)
                     ]
                     trans.append(
@@ -205,21 +198,31 @@
                             for at in (0, 1)
                         ]
                     )
+                return trans
+
+            def deposit(q, parity, psi=psi, place=place, col_at=col_at):
+                plane, window, rest = place(parity)
+                outof = lax.rem(col_at, LANES)
+                ahead = lane >= col_at
+                own_rows = slice(parity * half, (parity + 1) * half)
+                terms = ([], [])
                 for at in (0, 1):
-                    real, imag = q[parity][at]
-                    tr, ti = trans[0][at], trans[1][at]
-                    chi[position, 0, own_rows, spans[at]] = (tr * real + ti * imag).astype(chi.dtype)
-                    chi[position, 1, own_rows, spans[at]] = (tr * imag - ti * real).astype(chi.dtype)
-
-    def deeper(step, carry):
-        index = sections * own - 1 - step
-        layer_step(index // own, lax.rem(index, own), False)
-        return carry
-
-    lax.fori_loop(0, (sections - 1 - section) * own, deeper, 0)
-
-    def mine(step, carry):
-        layer_step(section, own - 1 - step, True)
+                    real, imag = q[at]
+                    psi_real, psi_imag = (plane_of[own_rows, spans[at]] for plane_of in psi)
+                    pair = psi_real * real + psi_imag * imag, psi_real * imag - psi_imag * real
+                    for part in (0, 1):
+                        terms[part].append(pltpu.roll(rows_later(pair[part], rest), outof, 1))
+                for part in (0, 1):
+                    left, right = terms[part]
+                    shifted = (
+                        jnp.where(ahead, left, 0.0),
+                        jnp.where(ahead, right, left),
+                        jnp.where(ahead, 0.0, right),
+                    )
+                    for at in range(3):
+                        totals[layer, part, plane, window, spans[at]] += shifted[at]
+
+            layer_step(position, chi, tables_ref, kernel_cos, kernel_sin, trans_of, deposit)
         return carry
 
     lax.fori_loop(0, own, mine, 0)
@@ -269,12 +272,27 @@
     pl.semaphore_wait(barrier, len(others))
 
 
-def gather_kernel(
+def descend_kernel(
     sections,
     bands,
+    offsets_ref,
     share_ref,
-    trans_ref,
-    local_sem,
+    residual_ref,
+    phase_ref,
+    amp_ref,
+    prop_ref,
+    tables_ref,
+    order_ref,
+    chi,
+    own_trans,
+    kernel_cos,
+    kernel_sin,
+    held,
+    layer_wide,
+    layer_trans,
+    pick_rows,
+    pick_cols,
+    woven,
     down_send,
     down_recv,
     plane_send,
@@ -285,12 +303,15 @@
     section, band = lax.axis_index("depth"), lax.axis_index("probe")
     chips = bands // 2
     chip, core = band // 2, band % 2
+    positions = residual_ref.shape[0]
+    own, _, band_rows, patch = share_ref.shape
+    last = sections - 1
     meet(section, band, sections, bands)
 
     def send(source, slot, to, send_sem, recv_sem):
         return pltpu.make_async_remote_copy(
             src_ref=source,
-            dst_ref=trans_ref.at[slot],
+            dst_ref=held.at[slot],
             send_sem=send_sem,
             recv_sem=recv_sem,
             device_id=to,
@@ -302,70 +323,154 @@
             share_ref, (origin, band), (target, band), down_send.at[target], down_recv.at[origin]
         )
 
-    def across(origin, j, source):
+    def across(origin, j):
         return send(
-            source,
+            held.at[origin, band],
             (origin, band),
             (section, 2 * ((chip + j) % chips) + core),
             plane_send.at[origin, j],
             plane_recv.at[origin, j],
         )
 
-    def to_pair(origin, j, source):
+    def to_pair(origin, j):
         slot = (origin, 2 * ((chip + chips - j) % chips) + core)
         return send(
-            source if j == 0 else trans_ref.at[slot],
+            held.at[slot],
             slot,
             (section, 2 * chip + 1 - core),
             pair_send.at[origin, j],
             pair_recv.at[origin, j],
         )
 
-    for target in range(sections - 1):
-
-        @pl.when(section > target)
-        def _(target=target):
-            down(target, section).start()
-
-    own_copy = pltpu.make_async_copy(share_ref, trans_ref.at[section, band], local_sem)
-    own_copy.start()
-    for j in range(1, chips):
-        across(section, j, share_ref).start()
-    to_pair(section, 0, share_ref).start()
-    for origin in range(1, sections):
-
-        @pl.when(section < origin)
-        def _(origin=origin):
-            down(0, origin).wait_recv()
-            held = trans_ref.at[origin, band]
-            for j in range(1, chips):
-                across(origin, j, held).start()
-            to_pair(origin, 0, held).start()
-
-    for origin in range(sections):
-
-        @pl.when(section <= origin)
-        def _(origin=origin):
-            for j in range(1, chips):
-                across(origin, j, share_ref).wait_recv()
-                to_pair(origin, j, None).start()
-
-    for origin in range(sections):
-
-        @pl.when(section <= origin)
-        def _(origin=origin):
-            for j in range(chips):
-                to_pair(origin, j, share_ref).wait()
-                if j:
-                    across(origin, j, share_ref).wait_send()
-
-    for target in range(sections - 1):
+    def fan_out(origin):
+        down(0, origin).wait_recv()
+        for j in range(1, chips):
+            across(origin, j).start()
+        to_pair(origin, 0).start()
+
+    def share_pair(origin):
+        for j in range(1, chips):
+            across(origin, j).wait_recv()
+            to_pair(origin, j).start()
+
+    def send_down():
+        for target in range(last):
+
+            @pl.when(section > target)
+            def _(target=target):
+                down(target, section).start()
+
+    @pl.when(section == last)
+    def _():
+        send_down()
+
+    split = order_ref[...]
+    exact = functools.partial(
+        lax.dot_general, precision=lax.Precision.HIGHEST, preferred_element_type=jnp.float32
+    )
+    order = split.astype(jnp.float32)
+    ordered = exact(order, prop_ref[...], (((1,), (0,)), ((), ())))
+    ordered = exact(ordered, order, (((1,), (1,)), ((), ())))
+    kernel_cos[...], kernel_sin[...] = cos_sin(ordered)
+    low = chi.dtype
+    width = chi.shape[2]
+    half = width // 2
+    row = lax.broadcasted_iota(jnp.int32, (width, patch), 0)
+    row_order = jnp.where(row < half, 2 * row, 2 * (row - half) + 1)
+    row_from = lax.broadcasted_iota(jnp.int32, (width, patch), 1) - row_order
+    col_from = lax.broadcasted_iota(jnp.int32, (patch, width), 0) - lax.broadcasted_iota(
+        jnp.int32, (patch, width), 1
+    )
+    for position in range(positions):
+        picked = jnp.where(row_from == offsets_ref[position, 0], 1.0, 0.0)
+        pick_rows[position] = picked.astype(low)
+        picked = jnp.where(col_from == offsets_ref[position, 1], 1.0, 0.0)
+        pick_cols[position] = picked.astype(low)
+        for part in (0, 1):
+            chi[position, part] = dot(split, residual_ref[position, part]).astype(low)
+
+    @pl.when(section < last)
+    def _():
+        fan_out(last)
+        send_down()
+
+    def own_layer(layer, carry):
+        for at, span in enumerate(spans_of(3)):
+            cosine, sine = cos_sin(phase_ref[layer, :, span])
+            amp = amp_ref[layer, :, span]
+            for part, field in enumerate((amp * cosine, amp * sine)):
+                woven[part, at] = field
+                for parity in (0, 1):
+                    own_trans[layer, part, parity, : patch // 2, span] = woven[
+                        part, at, pl.ds(parity, patch // 2, 2), :
+                    ]
+        for part in (0, 1):
+            for parity in (0, 1):
+                own_trans[layer, part, parity, patch // 2 :, :] = jnp.zeros(
+                    (SUBLANES, patch), jnp.float32
+                )
+        return carry
+
+    lax.fori_loop(0, own, own_layer, 0)
+    def fan_rest(step, carry):
+        fan_out(last - 1 - step)
+        return carry
+
+    @pl.when(section < last)
+    def _():
+        lax.fori_loop(0, last - 1 - section, fan_rest, 0)
+        share_pair(last)
+
+    def through(step, carry):
+        origin = last - step
+        for j in range(chips):
+            to_pair(origin, j).wait_recv()
+
+        def one_layer(step, carry):
+            layer = own - 1 - step
+            for part in (0, 1):
+                for from_band in range(bands):
+                    layer_wide[part, pl.ds(from_band * band_rows, band_rows), :] = held[
+                        origin, from_band, layer, part
+                    ].astype(jnp.float32)
+                layer_trans[:, part * patch : (part + 1) * patch] = layer_wide[part].astype(low)
+            for position in range(positions):
+                across_rows = dot(pick_rows[position], layer_trans[...]).astype(low)
+                window = [
+                    dot(across_rows[:, part * patch : (part + 1) * patch], pick_cols[position])
+                    for part in (0, 1)
+                ]
+
+                def trans_of(parity, window=window):
+                    own_rows = slice(parity * half, (parity + 1) * half)
+                    return [[plane[own_rows, span] for span in spans_of(2)] for plane in window]
+
+                layer_step(position, chi, tables_ref, kernel_cos, kernel_sin, trans_of)
+
+            @pl.when((step == 0) & (origin - 1 > section))
+            def _():
+                share_pair(origin - 1)
+
+            return carry
+
+        return lax.fori_loop(0, own, one_layer, carry)
+
+    lax.fori_loop(0, last - section, through, 0)
+
+    def settle(step, carry):
+        origin = last - step
+        for j in range(chips):
+            to_pair(origin, j).wait_send()
+            if j:
+                across(origin, j).wait_send()
+        return carry
+
+    lax.fori_loop(0, last - section, settle, 0)
+    for target in range(last):
 
         @pl.when(section > target)
         def _(target=target):
             down(target, section).wait_send()
-
-    own_copy.wait()
 
 
 def scatter_kernel(
@@ -490,7 +595,6 @@
     own, patch, _ = object_phase.shape
     sections = lax.axis_size("depth")
     bands = lax.axis_size("probe")
-    section = lax.axis_index("depth")
     band_rows = patch // bands
     chips = bands // 2
     assert width == 2 * LANES and patch == 3 * LANES
@@ -499,20 +603,31 @@
     phase = lax.dynamic_slice_in_dim(object_phase, start, band_rows, 1)
     amp = lax.dynamic_slice_in_dim(object_amp, start, band_rows, 1)
     share = jnp.stack([amp * jnp.cos(phase), amp * jnp.sin(phase)], 1).astype(jnp.bfloat16)
-    share = share.reshape(own, 2, band_rows // 2, 2, patch).swapaxes(2, 3)
-    share = share.reshape(own, 2, band_rows, patch)
 
     vmem = pl.BlockSpec(memory_space=pltpu.VMEM)
     smem = pl.BlockSpec(memory_space=pltpu.SMEM)
-    anywhere = pl.BlockSpec(memory_space=pl.ANY)
     dma = pltpu.SemaphoreType.DMA
-    trans = pl.pallas_call(
-        functools.partial(gather_kernel, sections, bands),
-        out_shape=jax.ShapeDtypeStruct((sections, bands) + share.shape, jnp.bfloat16),
-        in_specs=[anywhere],
-        out_specs=anywhere,
+    tables = jnp.asarray(half_tables(width))
+    order = jnp.asarray(order_table(width))
+    split_trans = (own, 2, 2, patch // 2 + SUBLANES, patch)
+    plane = jax.ShapeDtypeStruct((width, width), jnp.float32)
+    chi, own_trans, kernel_cos, kernel_sin = pl.pallas_call(
+        functools.partial(descend_kernel, sections, bands),
+        out_shape=(
+            jax.ShapeDtypeStruct(residual.shape, jnp.bfloat16),
+            jax.ShapeDtypeStruct(split_trans, jnp.float32),
+            plane,
+            plane,
+        ),
+        in_specs=[smem] + [vmem] * 7,
+        out_specs=(vmem,) * 4,
         scratch_shapes=[
-            dma,
+            pltpu.VMEM((sections, bands) + share.shape, jnp.bfloat16),
+            pltpu.VMEM((2, patch, patch), jnp.float32),
+            pltpu.VMEM((patch, 2 * patch), jnp.bfloat16),
+            pltpu.VMEM((positions, width, patch), jnp.bfloat16),
+            pltpu.VMEM((positions, patch, width), jnp.bfloat16),
+            pltpu.VMEM((2, 3, patch, LANES), jnp.float32),
             dma((sections,)),
             dma((sections,)),
             dma((sections, chips)),
@@ -520,39 +635,29 @@
             dma((sections, chips)),
             dma((sections, chips)),
         ],
-        compiler_params=pltpu.CompilerParams(collective_id=0, has_side_effects=True),
-        name="gather",
-    )(share)
+        compiler_params=pltpu.CompilerParams(
+            collective_id=0, has_side_effects=True, vmem_limit_bytes=VMEM_BYTES
+        ),
+        name="descend",
+    )(offsets, share, residual, object_phase, object_amp, prop_phase, tables, order)
 
     rows_each, cols_each = width // bands, width // sections
     grads, probe_sum = pl.pallas_call(
-        adjoint_kernel,
+        own_kernel,
         out_shape=(
             jax.ShapeDtypeStruct((bands, own, 2, band_rows, patch), jnp.bfloat16),
             jax.ShapeDtypeStruct((bands, 2, rows_each, width), jnp.bfloat16),
         ),
-        in_specs=[smem, smem] + [vmem] * 6,
+        in_specs=[smem] + [vmem] * 7,
         out_specs=(vmem, vmem),
         scratch_shapes=[
             pltpu.VMEM(residual.shape, jnp.bfloat16),
-            pltpu.VMEM((2, 2, patch // 2 + SUBLANES, patch), jnp.float32),
-            pltpu.VMEM((width, width), jnp.float32),
-            pltpu.VMEM((width, width), jnp.float32),
-            pltpu.VMEM((own, 2, 2, patch // 2 + SUBLANES, patch), jnp.float32),
+            pltpu.VMEM(split_trans, jnp.float32),
             pltpu.VMEM((3, patch, LANES), jnp.float32),
         ],
         compiler_params=pltpu.CompilerParams(vmem_limit_bytes=VMEM_BYTES),
-        name="adjoint",
-    )(
-        section.astype(jnp.int32)[None],
-        offsets,
-        residual,
-        saved_waves,
-        trans,
-        prop_phase,
-        jnp.asarray(half_tables(width)),
-        jnp.asarray(order_table(width)),
-    )
+        name="own",
+    )(offsets, chi, saved_waves, own_trans, kernel_cos, kernel_sin, tables, order)
     block_g, block_p = (own, 2, band_rows, patch), (2, rows_each, width)
     low = jnp.bfloat16
     return pl.pallas_call(

time: 96.5 us -> 95.3 us (0.988)
  Pallas kernels: 88.8 us -> 87.7 us
    another operation x1 -> x2, other arithmetic: 0.68 us -> 2.2 us  [shards(): jnp.stack([amp * jnp.cos(phase), amp * jnp.sin(phase)], 1)]
    another operation x1 -> x0, other arithmetic: 1.52 us -> none
    pallas_call x2, Pallas kernels: 71.4 us -> 69.9 us  [the longest x1 57.6 us: shards(): pl.pallas_call(functools.partial(descend_kernel, sections, bands), out_sh...]
where the time goes in v3:
time: 95.3 us; the launch traced here: 95 us
  Pallas kernels  87.7 us (92%)
  local copies, waits for them, and re-layouts  4.41 us (5%)
  other arithmetic  2.2 us (2%)
    pallas_call x1, Pallas kernels, shards(): pl.pallas_call(functools.partial(descend_kernel, sections, bands), out_sh...  57.6 us
    pallas_call x1, Pallas kernels, shards(): pl.pallas_call(functools.partial(scatter_kernel, sections, bands), out_sh...  17.8 us
    pallas_call x1, Pallas kernels, shards(): pl.pallas_call(own_kernel, out_shape=(jax.ShapeDtypeStruct((bands, own, 2...  12.4 us
    unnamed x3, local copies, waits for them, and re-layouts  4.41 us
    another operation x2, other arithmetic, shards(): jnp.stack([amp * jnp.cos(phase), amp * jnp.sin(phase)], 1)  2.2 us

profile of v3, /device:TPU:0, one launch (start us, length us, event | category | flops | bytes accessed | tf_op | source)
XLA Modules:
  0.0 95.0 jit_solution(2934173018604332805)
XLA Ops:
  0.6 1.3 %copy.12.offsets_ref = s32[4,2]{1,0:T(4,128)} copy(s32[4,2]{0,1:T(2,128)} %param.13) | data formatting | bytes 64 | tf_op args[5]
  2.0 1.5 %fusion = (bf16[2,1,48,384]{3,2,1,0:T(8,128)(2,1)S(1)}, bf16[2,1,48,384]{3,2,1,0:T(8,128)(2,1)S(1)}) fusion(f32[2,384,384]{2,1,0:T(8,128)} %phase_ref.1, s32[]{:T(128)S(6)} %select_n.4, f32[2,384,384]{2,1,0:T(8,128)} %amp_ref.1), kind=kLoop, calls=%fused_computation.3 | loop fusion | flops 147456 | bytes 442372 | tf_op jit(solution)/shard_map/stack | solution.py:605
  3.5 0.7 pad_maximum_fusion.share_ref
  4.2 57.6 %descend.1 = (bf16[4,2,256,256]{3,2,1,0:T(8,128)(2,1)}, f32[2,2,2,200,384]{4,3,2,1,0:T(8,128)}, f32[256,256]{1,0:T(8,128)}, f32[256,256]{1,0:T(8,128)}) custom-call(s32[4,2]{1,0:T(4,128)} %copy.12.offsets_ref, bf16[2,2,48,384]{3,2,1,0:T(8,128)(2,1)} %pad_maximum_fusion.share_ref, bf16[4,2,256,256]{3,2,1,0:T(8,128)(2,1)} %residual_ref.1, ...), custom_call_target="tpu_custom_call" | custom-call | tf_op jit(solution)/shard_map/descend/pallas_call | solution.py:614
  61.8 12.4 %own.1 = (bf16[8,2,2,48,384]{4,3,2,1,0:T(8,128)(2,1)}, bf16[8,2,32,256]{3,2,1,0:T(8,128)(2,1)}) custom-call(s32[4,2]{1,0:T(4,128)} %copy.12.offsets_ref, bf16[4,2,256,256]{3,2,1,0:T(8,128)(2,1)} %get-tuple-element.8.chi_ref, bf16[2,4,2,256,256]{4,3,2,1,0:T(8,128)(2,1)} %waves_ref.1, f32[2,2,2,200,384]{4,3,2,1,0:T(8,128)} %get-tuple-element.9.trans_ref, ...), custom_call_target="tpu_custom_call" | custom-call | tf_op jit(solution)/shard_map/own/pallas_call | solution.py:645
  74.1 17.8 %scatter.1 = (f32[2,2,48,384]{3,2,1,0:T(8,128)}, f32[2,32,64]{2,1,0:T(8,128)}) custom-call(bf16[8,2,2,48,384]{4,3,2,1,0:T(8,128)(2,1)} %get-tuple-element.12.grads_ref, bf16[8,2,32,256]{3,2,1,0:T(8,128)(2,1)} %get-tuple-element.13.probe_ref), custom_call_target="tpu_custom_call" | custom-call | tf_op jit(solution)/shard_map/scatter/pallas_call | solution.py:663
  91.9 1.7 %copy.15 = f32[2,2,48,384]{3,2,1,0:T(8,128)} copy(f32[2,2,48,384]{3,2,1,0:T(8,128)} %get-tuple-element.18) | data formatting | bytes 589824
  93.6 1.4 %copy.16 = f32[2,32,64]{2,1,0:T(8,128)} copy(f32[2,32,64]{2,1,0:T(8,128)} %get-tuple-element.19) | data formatting | bytes 32768
